TPU v7x, 256 devices: a whole 4x4x8 slice. The times are simulated.
256 devices in a mesh: dp: 4 (over y), vocab: 64 (over x, z, core).
Axes of the slice: x: 4, y: 4, z: 8, core: 2. Of those that a mesh axis runs over, the one named last changes fastest.
Arguments:
- window_hidden_states: bfloat16 [1024, 4608], P('dp'), may hold values from -40 to 40
- output_head_weight: bfloat16 [196608, 4608], P(('dp', 'vocab')), may hold values from -0.044194174 to 0.044194174
- adapter_first_factor: bfloat16 [64, 4608], replicated, may hold values from -0.09375 to 0.09375
- adapter_second_factor: bfloat16 [196608, 64], P(('dp', 'vocab')), may hold values from -0.1875 to 0.1875
- first_factor_direction: bfloat16 [64, 4608], replicated, may hold values from -0.09375 to 0.09375
- second_factor_direction: bfloat16 [196608, 64], P(('dp', 'vocab')), may hold values from -0.75 to 0.75
Outputs:
- grad_a: float32 [64, 4608], replicated
- grad_b: float32 [196608, 64], P(('dp', 'vocab'))
All inputs are finite; a program needn't handle non-finite values.
Results may differ from a plain program's by a relative error of at most 0.007.
Values may be sent and summed in bfloat16 or wider, within the bound.
A program may use at most 128 MiB of HBM per device.

v0:
```python
import jax
import jax.numpy as jnp
from jax import lax
from jax.sharding import PartitionSpec as P


def wide_stats(vocab_logits, tangent_logits):
    row_top = lax.pmax(jnp.max(vocab_logits, axis=1), ("dp", "vocab"))
    exp_terms = jnp.exp(vocab_logits - row_top[:, None])
    row_total, row_weighted = lax.psum(
        (jnp.sum(exp_terms, axis=1), jnp.sum(exp_terms * tangent_logits, axis=1)), ("dp", "vocab")
    )
    return (row_top, row_total, row_weighted)


def output_head_logits(
    states, reduced_rank_projection, low_tangent, weights, factor, factor_tangent
):
    vocab_logits = jnp.dot(states, weights.T, preferred_element_type=jnp.float32)
    vocab_logits = vocab_logits + jnp.dot(
        reduced_rank_projection, factor.T, preferred_element_type=jnp.float32
    )
    tangent_logits = jnp.dot(low_tangent, factor.T, preferred_element_type=jnp.float32)
    tangent_logits = tangent_logits + jnp.dot(
        reduced_rank_projection, factor_tangent.T, preferred_element_type=jnp.float32
    )
    return (vocab_logits, tangent_logits)


def hessian_rows(vocab_logits, tangent_logits, row_top, row_total, row_weighted):
    probs = jnp.exp(vocab_logits - row_top[:, None]) / row_total[:, None]
    row_mean = row_weighted / row_total
    return (probs * (tangent_logits - row_mean[:, None])).astype(jnp.bfloat16)


def shards(
    window_hidden_states,
    output_head_weight,
    adapter_first_factor,
    adapter_second_factor,
    first_factor_direction,
    second_factor_direction,
):
    reduced_rank_projection = jnp.dot(
        window_hidden_states, adapter_first_factor.T, preferred_element_type=jnp.float32
    ).astype(jnp.bfloat16)
    low_tangent = jnp.dot(
        window_hidden_states, first_factor_direction.T, preferred_element_type=jnp.float32
    ).astype(jnp.bfloat16)
    gathered_states, gathered_rank, gathered_tangent = (
        lax.all_gather(window_hidden_states, "dp", axis=0, tiled=True),
        lax.all_gather(reduced_rank_projection, "dp", axis=0, tiled=True),
        lax.all_gather(low_tangent, "dp", axis=0, tiled=True),
    )
    vocab_logits, tangent_logits = output_head_logits(
        gathered_states,
        gathered_rank,
        gathered_tangent,
        output_head_weight,
        adapter_second_factor,
        second_factor_direction,
    )
    row_top, row_total, row_weighted = wide_stats(vocab_logits, tangent_logits)
    curvature_product = hessian_rows(vocab_logits, tangent_logits, row_top, row_total, row_weighted)
    grad_b = jnp.dot(curvature_product.T, gathered_rank, preferred_element_type=jnp.float32)
    column_sum = lax.psum(
        jnp.dot(curvature_product, adapter_second_factor, preferred_element_type=jnp.float32),
        ("dp", "vocab"),
    )
    column_round = column_sum.astype(jnp.bfloat16)
    grad_a = jnp.dot(column_round.T, gathered_states, preferred_element_type=jnp.float32)
    return (grad_a, grad_b)


def solution(mesh):
    in_specs = (
        P("dp", None),
        P(("dp", "vocab"), None),
        P(),
        P(("dp", "vocab"), None),
        P(),
        P(("dp", "vocab"), None),
    )
    out_specs = (P(), P(("dp", "vocab"), None))
    return jax.shard_map(shards, mesh=mesh, in_specs=in_specs, out_specs=out_specs, check_vma=False)
```

profile of v0, /device:TPU:1, one launch (start us, length us, event | category | flops | bytes accessed | tf_op | source)
XLA Modules:
  0.0 375.8 jit_solution(1615872188829419691)
XLA Ops:
  7.2 0.0 copy-start
  7.2 0.0 copy-start.1
  7.2 0.0 all-gather.2.cloned.1.call-start
  7.2 0.7 all-gather.2.cloned.1.call-update
  7.9 0.3 copy-done
  8.2 0.0 copy-start.4
  8.2 0.0 copy-start.2
  8.2 2.6 convolution_convert_fusion.1
  10.8 10.6 %all_gather.10 = bf16[1024,64]{0,1:T(8,128)(2,1)S(1)} all-gather(bf16[256,64]{0,1:T(8,128)(2,1)S(1)} %convolution_convert_fusion.1), channel_id=1, replica_groups=mesh['dp'=4,'vocab'=64] {'dp'}, dimensions={0}, use_global_device_ids=true | all-gather | bytes 163840 | tf_op jit(solution)/shard_map/all_gather | solution.py:52
  21.4 0.0 copy-done.1
  21.4 0.0 copy-done.4
  21.4 0.7 convolution_convert_fusion
  22.1 9.4 %all_gather.11 = bf16[1024,64]{1,0:T(8,128)(2,1)S(1)} all-gather(bf16[256,64]{1,0:T(8,128)(2,1)S(1)} %convolution_convert_fusion), channel_id=1, replica_groups=mesh['dp'=4,'vocab'=64] {'dp'}, dimensions={0}, use_global_device_ids=true | all-gather | bytes 163840 | tf_op jit(solution)/shard_map/all_gather | solution.py:53
  31.5 0.0 copy-done.2
  31.5 2.3 fusion.5
  33.8 75.3 %all-gather.2.cloned.1.call-done = bf16[1024,4608]{1,0:T(8,128)(2,1)} async-done(((bf16[256,4608]{1,0:T(8,128)(2,1)}), bf16[1024,4608]{1,0:T(8,128)(2,1)}) %all-gather.2.cloned.1.call-update) | async-done | bytes 9437200 | tf_op jit(solution)/shard_map/all_gather | solution.py:51
  109.1 12.1 %fusion.4 = f32[1024,768]{0,1:T(8,128)S(1)} fusion(bf16[1024,4608]{1,0:T(8,128)(2,1)} %all-gather.2.cloned.1.call-done, bf16[768,4608]{1,0:T(8,128)(2,1)} %param.7), kind=kOutput, calls=%fused_computation.11 | convolution fusion | flops 7247757312 | bytes 19660800 | tf_op jit(solution)/shard_map/dot_general | solution.py:19
  121.3 0.0 copy-start.3
  121.3 2.2 fusion.3
  123.5 77.1 %pmax.7 = f32[1024]{0:T(1024)S(1)} all-reduce(f32[1024]{0:T(1024)S(1)} %get-tuple-element.6), channel_id=1, replica_groups=mesh['dp'=4,'vocab'=64] {'dp','vocab'}, use_global_device_ids=true, to_apply=%region_1.0 | all-reduce | flops 1024 | bytes 8192 | tf_op jit(solution)/shard_map/pmax | solution.py:8
  200.7 0.0 copy-done.3
  200.7 5.4 %fusion = (f32[1024]{0:T(1024)S(1)}, f32[1024]{0:T(1024)S(1)}, f32[1024,768]{0,1:T(8,128)}) fusion(f32[1024,768]{0,1:T(8,128)} %get-tuple-element.7, f32[1024]{0:T(1024)S(1)} %pmax.7, f32[1024,768]{0,1:T(8,128)} %fusion.5, bf16[1024,64]{0,1:T(8,128)(2,1)S(1)} %all_gather.10, bf16[768,64]{0,1:T(8,128)(2,1)S(1)} %copy-done.3), kind=kOutput, calls=%fused_computation.3 | convolution fusion | flops 104593408 | bytes 9678848 | tf_op jit(solution)/shard_map/dot_general | solution.py:24
  206.1 73.7 %all-reduce = (f32[1024]{0:T(1024)S(1)}, f32[1024]{0:T(1024)S(1)}) all-reduce(f32[1024]{0:T(1024)S(1)} %get-tuple-element.3, f32[1024]{0:T(1024)S(1)} %get-tuple-element.2), channel_id=1, replica_groups=mesh['dp'=4,'vocab'=64] {'dp','vocab'}, use_global_device_ids=true, to_apply=%region_5.0 | all-reduce | flops 2048 | bytes 16384 | tf_op jit(solution)/shard_map/psum | solution.py:10
  279.9 3.7 multiply_convert_fusion
  283.6 1.3 fusion.7
  284.8 0.6 fusion.6
  285.4 77.0 %all-reduce.2 = bf16[1024,64]{1,0:T(8,128)(2,1)S(1)} all-reduce(f32[1024,64]{1,0:T(8,128)S(1)} %fusion.6), channel_id=1, replica_groups=mesh['dp'=4,'vocab'=64] {'dp','vocab'}, use_global_device_ids=true, to_apply=%region_6.0 | all-reduce | flops 65536 | bytes 393216 | tf_op jit(solution)/shard_map/psum | solution.py:66
  362.5 6.5 %fusion.8 = f32[64,4608]{1,0:T(8,128)} fusion(bf16[1024,64]{1,0:T(8,128)(2,1)S(1)} %all-reduce.2, bf16[1024,4608]{1,0:T(8,128)(2,1)} %all-gather.2.cloned.1.call-done), kind=kOutput, calls=%fused_computation.15 | convolution fusion | flops 603979776 | bytes 10747904 | tf_op jit(solution)/shard_map/dot_general | solution.py:71
  (1 shorter events, 0.0 us)
Async XLA Ops:
  7.2 1.1 copy-start
  7.2 14.2 %copy-start.1 = (bf16[256,4608]{1,0:T(8,128)(2,1)S(1)}, bf16[256,4608]{1,0:T(8,128)(2,1)}, u32[]{:S(2)}) copy-start(bf16[256,4608]{1,0:T(8,128)(2,1)} %param.6) | copy-start | bytes 7077892
  7.2 101.9 %all-gather.2.cloned.1.call-start = ((), (), s32[]{:S(2)}) async-start(), calls=%async_computation | async-start | bytes 11796480 | tf_op jit(solution)/shard_map/all_gather | solution.py:51
  8.2 13.1 %copy-start.4 = (bf16[64,4608]{1,0:T(8,128)(2,1)S(1)}, bf16[64,4608]{1,0:T(8,128)(2,1)}, u32[]{:S(2)}) copy-start(bf16[64,4608]{1,0:T(8,128)(2,1)} %param.10) | copy-start | bytes 1769476
  8.2 23.3 %copy-start.2 = (bf16[768,64]{0,1:T(8,128)(2,1)S(1)}, bf16[768,64]{0,1:T(8,128)(2,1)}, u32[]{:S(2)}) copy-start(bf16[768,64]{0,1:T(8,128)(2,1)} %param.9) | copy-start | bytes 294916
  121.3 79.4 %copy-start.3 = (bf16[768,64]{0,1:T(8,128)(2,1)S(1)}, bf16[768,64]{0,1:T(8,128)(2,1)}, u32[]{:S(2)}) copy-start(bf16[768,64]{0,1:T(8,128)(2,1)} %param.11) | copy-start | bytes 294916
Sparse Core Ops, SparseCore 0:
  9.8 99.2 all-gather.1
where the time goes:
time: 376 us
  blocking collectives  248 us (66%)
  waiting for transfers between devices  76 us (20%)
  matrix products  33.8 us (9%)
  between operations  14.1 us (4%)
    pmax x1, blocking collectives, wide_stats(): row_top = lax.pmax(jnp.max(vocab_logits, axis=1), ('dp', 'vocab'))  77.1 us
    psum x1, blocking collectives, shards(): lax.psum(jnp.dot(curvature_product, adapter_second_factor, preferred_elem...  77 us
    all_gather x1, waiting for transfers between devices, shards(): lax.all_gather(window_hidden_states, 'dp', axis=0, tiled=True)  75.3 us
    psum x1, blocking collectives, wide_stats(): lax.psum((jnp.sum(exp_terms, axis=1), jnp.sum(exp_terms * tangent_logits,...  73.7 us
    dot_general x1, matrix products, output_head_logits(): jnp.dot(states, weights.T, preferred_element_type=jnp.float32)  12.1 us
    all_gather x1, blocking collectives, shards(): lax.all_gather(reduced_rank_projection, 'dp', axis=0, tiled=True)  10.6 us
    all_gather x1, blocking collectives, shards(): lax.all_gather(low_tangent, 'dp', axis=0, tiled=True)  9.37 us
  transfers between devices with their start and end apart: 1, of which 1 were waited for; matrix products, arithmetic and copies ran while one was open for 1% of the time, Pallas kernels for 0%

commit v1 on v0

v1 whole, which is shorter than its diff:
```python
import jax
import jax.numpy as jnp
from jax import lax
from jax.experimental import pallas as pl
from jax.experimental.pallas import tpu as pltpu
from jax.sharding import PartitionSpec as P

MESH = pl.DeviceIdType.MESH
F32 = jnp.float32
BF16 = jnp.bfloat16

WIDTH = 4608
RANK = 64
VOCAB = 768
TOKENS = 1024
CHUNK = 256
ROWS = VOCAB + 2 * RANK
NX, NY, NZ = 4, 4, 8
DEPTH = 1536
BLOCK = 64
COLS = 512


def place(x, y, z, c):
    return (y, x * 16 + z * 2 + c)


def remote(src, dst, send_sem, recv_sem, device):
    return pltpu.make_async_remote_copy(
        src_ref=src,
        dst_ref=dst,
        send_sem=send_sem,
        recv_sem=recv_sem,
        device_id=device,
        device_id_type=MESH,
    )


def merge(parts):
    top = parts[0][0]
    for part in parts[1:]:
        top = jnp.maximum(top, part[0])
    scales = [jnp.exp(part[0] - top) for part in parts]
    total = scales[0] * parts[0][1]
    weighted = total * parts[0][2]
    for scale, part in zip(scales[1:], parts[1:]):
        share = scale * part[1]
        total = total + share
        weighted = weighted + share * part[2]
    mean = weighted / total
    moved = None
    plain = None
    for scale, part in zip(scales, parts):
        shift = scale * (part[2] - mean)
        one = scale * part[3] + shift * part[4]
        two = scale * part[4]
        moved = one if moved is None else moved + one
        plain = two if plain is None else plain + two
    return top, total, mean, moved, plain


def stat_rows(top, total, mean):
    return jnp.concatenate([top, total, mean, jnp.zeros((5, top.shape[1]), F32)], axis=0)


def kernel(
    s_ref, w_ref, a_ref, ad_ref, bt_ref, dbt_ref, ga_ref, gb_ref,
    wall, sg, acc, e_buf, t_buf, xr, bl, bt2, h1, h2, hs, cfull,
    p0, r1, p1, r2, r3, cg, stg,
    load_sem, ys, yr, gs, gr, ss1, sr1, xs, xrv, zs, zr, cs, cr, ts, tr, fs, fr,
):
    y = lax.axis_index("dp")
    v = lax.axis_index("vocab")
    x, z, c = v // 16, (v // 2) % 8, v % 2
    sib = place(x, y, z, 1 - c)
    y_up, y_down = place(x, (y + 1) % NY, z, c), place(x, (y + 3) % NY, z, c)
    pairs = [(dx, dy) for dx in range(NX) for dy in range(NY) if (dx, dy) != (0, 0)]
    xy = [((x + dx) % NX, (y + dy) % NY) for dx, dy in pairs]

    barrier = pltpu.get_barrier_semaphore()
    everyone = [sib] + [place(px, py, z, c) for px, py in xy] + [place(x, y, (z + d) % NZ, c) for d in range(1, NZ)]
    for peer in everyone:
        pl.semaphore_signal(barrier, 1, device_id=peer, device_id_type=MESH)

    def rows_of(j, start, size):
        return sg.at[pl.ds(pl.multiple_of(j * CHUNK + start, 16), size)]

    loads = [
        pltpu.make_async_copy(s_ref, rows_of(y, 0, CHUNK), load_sem.at[0]),
        pltpu.make_async_copy(w_ref, wall.at[pl.ds(0, VOCAB)], load_sem.at[1]),
        pltpu.make_async_copy(a_ref, wall.at[pl.ds(VOCAB, RANK)], load_sem.at[2]),
        pltpu.make_async_copy(ad_ref, wall.at[pl.ds(VOCAB + RANK, RANK)], load_sem.at[3]),
    ]
    for load in loads:
        load.start()

    bt = bt_ref[...].astype(F32)
    dbt = dbt_ref[...].astype(F32)
    bl[...] = jnp.concatenate([bt, jnp.zeros_like(bt)], axis=0).T.astype(BF16)
    bt2[...] = jnp.concatenate([dbt, bt], axis=0).T.astype(BF16)

    pl.semaphore_wait(barrier, len(everyone))

    half = c * (CHUNK // 2)
    quarter = CHUNK // 4
    before, after, across = (y + 3) % NY, (y + 1) % NY, (y + 2) % NY
    mine = s_ref.at[pl.ds(pl.multiple_of(half, 16), CHUNK // 2)]
    sends = [
        remote(mine, rows_of(y, half, CHUNK // 2), ys.at[0], yr.at[0], y_up),
        remote(mine, rows_of(y, half, CHUNK // 2), ys.at[1], yr.at[1], y_down),
    ]
    for send in sends:
        send.start()

    def arrived(ref, send_sem, recv_sem):
        remote(ref, ref, send_sem, recv_sem, sib).wait_recv()

    def pass_on(j, k):
        held = rows_of(j, half, CHUNK // 2)
        copy = remote(held, held, gs.at[k], gr.at[k], sib)
        copy.start()
        sends.append(copy)

    def whole(j, k):
        arrived(rows_of(j, CHUNK // 2 - half, CHUNK // 2), gs.at[k], gr.at[k])

    def compute(j):
        first = pl.multiple_of(j * CHUNK, CHUNK)
        here = pl.ds(first, CHUNK)

        def deep(k, carry):
            at = pl.ds(pl.multiple_of(k * DEPTH, 128), DEPTH)
            part = lax.dot_general(wall[:, at], sg[here, at], (((1,), (1,)), ((), ())), preferred_element_type=F32)

            @pl.when(k == 0)
            def _():
                acc[...] = part

            @pl.when(k > 0)
            def _():
                acc[...] += part

            return carry

        lax.fori_loop(0, WIDTH // DEPTH, deep, 0)
        xr[:, here] = acc[VOCAB:ROWS, :].astype(BF16)

        def logits(i, top):
            at = pl.ds(pl.multiple_of(i * BLOCK, BLOCK), BLOCK)
            low = xr[:, here]
            row = acc[at, :] + jnp.dot(bl[at, :], low, preferred_element_type=F32)
            e_buf[at, here] = row
            t_buf[at, here] = jnp.dot(bt2[at, :], low, preferred_element_type=F32)
            return jnp.maximum(top, jnp.max(row.reshape(BLOCK // 8, 8, CHUNK), axis=0))

        top = lax.fori_loop(0, VOCAB // BLOCK, logits, jnp.full((8, CHUNK), -jnp.inf, F32))
        top = jnp.max(top, axis=0, keepdims=True)

        def sums(i, carry):
            at = pl.ds(pl.multiple_of(i * BLOCK, BLOCK), BLOCK)
            e = jnp.exp(e_buf[at, here] - top)
            e_buf[at, here] = e
            et = e * t_buf[at, here]
            return (
                carry[0] + jnp.sum(e.reshape(BLOCK // 8, 8, CHUNK), axis=0),
                carry[1] + jnp.sum(et.reshape(BLOCK // 8, 8, CHUNK), axis=0),
            )

        zero = jnp.zeros((8, CHUNK), F32)
        total, weighted = lax.fori_loop(0, VOCAB // BLOCK, sums, (zero, zero))
        total = jnp.sum(total, axis=0, keepdims=True)
        mean = jnp.sum(weighted, axis=0, keepdims=True) / total

        def rounded(i, carry):
            at = pl.ds(pl.multiple_of(i * BLOCK, BLOCK), BLOCK)
            e = e_buf[at, here]
            h1[at, :] = (e * (t_buf[at, here] - mean)).astype(BF16)
            h2[at, :] = e.astype(BF16)
            return carry

        lax.fori_loop(0, VOCAB // BLOCK, rounded, 0)
        side, there = j // 2, pl.ds(pl.multiple_of((j % 2) * CHUNK, CHUNK), CHUNK)
        p0[side, 0:RANK, there] = jnp.dot(bt_ref[...], h1[...], preferred_element_type=F32)
        p0[side, RANK : 2 * RANK, there] = jnp.dot(bt_ref[...], h2[...], preferred_element_type=F32)
        p0[side, 2 * RANK : 2 * RANK + 8, there] = stat_rows(top, total, mean)

    for load in loads:
        load.wait()
    compute(y)
    arrived(rows_of(before, half, CHUNK // 2), ys.at[0], yr.at[0])
    held = rows_of(before, half, quarter)
    sends.append(remote(held, held, ys.at[2], yr.at[2], y_up))
    sends[-1].start()
    pass_on(before, 0)
    arrived(rows_of(after, half, CHUNK // 2), ys.at[1], yr.at[1])
    held = rows_of(after, half + quarter, quarter)
    sends.append(remote(held, held, ys.at[3], yr.at[3], y_down))
    sends[-1].start()
    pass_on(after, 1)
    whole(before, 0)
    compute(before)
    whole(after, 1)
    compute(after)
    arrived(rows_of(across, half, quarter), ys.at[2], yr.at[2])
    arrived(rows_of(across, half + quarter, quarter), ys.at[3], yr.at[3])
    pass_on(across, 2)
    whole(across, 2)
    compute(across)

    copy = remote(p0.at[1 - c], r1, ss1.at[0], sr1.at[0], sib)
    copy.start()
    sends.append(copy)
    copy.wait_recv()
    for tx in range(NX):
        lanes = pl.ds(tx * 128, 128)

        def stats(ref, row):
            return ref[pl.ds(row, 1), lanes]

        own, other = p0.at[c], r1
        for ty in range(NY):
            g1, g2 = pl.ds(ty * 16, 16), pl.ds(RANK + ty * 16, 16)
            out = merge(
                [
                    (stats(ref, 128), stats(ref, 129), stats(ref, 130), ref[g1, lanes], ref[g2, lanes])
                    for ref in (own, other)
                ]
            )
            p1[tx * NY + ty] = jnp.concatenate([out[3], out[4], stat_rows(*out[:3])], axis=0)

    def unpack(ref, k):
        return (ref[k, 32:33], ref[k, 33:34], ref[k, 34:35], ref[k, 0:16], ref[k, 16:32])

    me = x * NY + y
    copies = []
    for k, (px, py) in enumerate(xy):
        copies.append(remote(p1.at[px * NY + py], r2.at[me], xs.at[k], xrv.at[k], place(px, py, z, c)))
        copies[-1].start()
    sends += copies
    r2[me] = p1[me]
    for k, (dx, dy) in enumerate(pairs):
        origin = ((x - dx + NX) % NX) * NY + (y - dy + NY) % NY
        arrived(r2.at[origin], xs.at[k], xrv.at[k])
    out = merge([unpack(r2, k) for k in range(NX * NY)])
    r3[z] = jnp.concatenate([out[3], out[4], stat_rows(*out[:3])], axis=0)
    for d in range(1, NZ):
        copy = remote(r3.at[z], r3.at[z], zs.at[d - 1], zr.at[d - 1], place(x, y, (z + d) % NZ, c))
        copy.start()
        sends.append(copy)
    for d in range(1, NZ):
        arrived(r3.at[(z - d + NZ) % NZ], zs.at[d - 1], zr.at[d - 1])
    top, total, mean, moved, plain = merge([unpack(r3, k) for k in range(NZ)])

    slot = c * NX + x
    strip = cg.at[slot, pl.ds(pl.multiple_of(y * 16, 16), 16)]
    strip[...] = (moved / total).astype(BF16)
    stg[slot] = stat_rows(top, total, mean)
    for d in range(1, NX):
        copy = remote(stg.at[slot], stg.at[slot], ts.at[d - 1], tr.at[d - 1], place((x + d) % NX, y, z, c))
        copy.start()
        sends.append(copy)
    for k, (px, py) in enumerate(xy):
        copy = remote(strip, strip, cs.at[k], cr.at[k], place(px, py, z, c))
        copy.start()
        sends.append(copy)
    for d in range(1, NX):
        arrived(stg.at[c * NX + (x - d + NX) % NX], ts.at[d - 1], tr.at[d - 1])
    held = stg.at[pl.ds(c * NX, NX)]
    copy = remote(held, held, fs.at[0], fr.at[0], sib)
    copy.start()
    sends.append(copy)
    for k, (dx, dy) in enumerate(pairs):
        from_x, from_y = (x - dx + NX) % NX, (y - dy + NY) % NY
        arrived(cg.at[c * NX + from_x, pl.ds(pl.multiple_of(from_y * 16, 16), 16)], cs.at[k], cr.at[k])
    held = cg.at[pl.ds(c * NX, NX)]
    copy = remote(held, held, fs.at[1], fr.at[1], sib)
    copy.start()
    sends.append(copy)
    arrived(stg.at[pl.ds((1 - c) * NX, NX)], fs.at[0], fr.at[0])

    factors, means = [], []
    for t in range(8):
        local_top = p0[t // 4, 128:129, (t % 4) * 128 : (t % 4 + 1) * 128]
        factors.append(jnp.exp(local_top - stg[t, 0:1]) / stg[t, 1:2])
        means.append(stg[t, 2:3])

    def hessian(i, carry):
        at = pl.ds(pl.multiple_of(i * BLOCK, BLOCK), BLOCK)
        for t in range(8):
            lanes = pl.ds(t * 128, 128)
            probs = e_buf[at, lanes] * factors[t]
            hs[at, lanes] = (probs * (t_buf[at, lanes] - means[t])).astype(BF16)
        return carry

    lax.fori_loop(0, VOCAB // BLOCK, hessian, 0)
    gb_ref[...] = lax.dot_general(xr[0:RANK, :], hs[...], (((1,), (1,)), ((), ())), preferred_element_type=F32)

    arrived(cg.at[pl.ds((1 - c) * NX, NX)], fs.at[1], fr.at[1])
    for t in range(8):
        cfull[:, t * 128 : (t + 1) * 128] = cg[t]

    def outer(n, carry):
        at = pl.ds(pl.multiple_of(n * COLS, 128), COLS)
        ga_ref[:, at] = jnp.dot(cfull[...], sg[:, at], preferred_element_type=F32)
        return carry

    lax.fori_loop(0, WIDTH // COLS, outer, 0)
    for send in sends:
        send.wait_send()


def shards(states, weight, first, second, first_direction, second_direction):
    vmem = pl.BlockSpec(memory_space=pltpu.VMEM)
    hbm = pl.BlockSpec(memory_space=pl.ANY)
    dma = pltpu.SemaphoreType.DMA
    grad_a, grad_b = pl.pallas_call(
        kernel,
        out_shape=(jax.ShapeDtypeStruct((RANK, WIDTH), F32), jax.ShapeDtypeStruct((RANK, VOCAB), F32)),
        in_specs=[hbm, hbm, hbm, hbm, vmem, vmem],
        out_specs=(vmem, vmem),
        scratch_shapes=[
            pltpu.VMEM((ROWS, WIDTH), BF16),
            pltpu.VMEM((TOKENS, WIDTH), BF16),
            pltpu.VMEM((ROWS, CHUNK), F32),
            pltpu.VMEM((VOCAB, TOKENS), F32),
            pltpu.VMEM((VOCAB, TOKENS), F32),
            pltpu.VMEM((2 * RANK, TOKENS), BF16),
            pltpu.VMEM((VOCAB, 2 * RANK), BF16),
            pltpu.VMEM((VOCAB, 2 * RANK), BF16),
            pltpu.VMEM((VOCAB, CHUNK), BF16),
            pltpu.VMEM((VOCAB, CHUNK), BF16),
            pltpu.VMEM((VOCAB, TOKENS), BF16),
            pltpu.VMEM((RANK, TOKENS), BF16),
            pltpu.VMEM((2, 2 * RANK + 8, TOKENS // 2), F32),
            pltpu.VMEM((2 * RANK + 8, TOKENS // 2), F32),
            pltpu.VMEM((NX * NY, 40, 128), F32),
            pltpu.VMEM((NX * NY, 40, 128), F32),
            pltpu.VMEM((NZ, 40, 128), F32),
            pltpu.VMEM((2 * NX, RANK, 128), BF16),
            pltpu.VMEM((2 * NX, 8, 128), F32),
            dma((4,)),
            dma((4,)), dma((4,)),
            dma((3,)), dma((3,)),
            dma((1,)), dma((1,)),
            dma((15,)), dma((15,)),
            dma((7,)), dma((7,)),
            dma((15,)), dma((15,)),
            dma((3,)), dma((3,)),
            dma((2,)), dma((2,)),
        ],
        compiler_params=pltpu.CompilerParams(
            collective_id=0, has_side_effects=True, vmem_limit_bytes=56 * 1024 * 1024
        ),
        cost_estimate=pl.CostEstimate(flops=10_000_000_000, bytes_accessed=20_000_000, transcendentals=800_000),
    )(states, weight, first, first_direction, second.T, second_direction.T)
    return grad_a, grad_b.T


def solution(mesh):
    in_specs = (
        P("dp", None),
        P(("dp", "vocab"), None),
        P(),
        P(("dp", "vocab"), None),
        P(),
        P(("dp", "vocab"), None),
    )
    out_specs = (P(), P(("dp", "vocab"), None))
    return jax.shard_map(shards, mesh=mesh, in_specs=in_specs, out_specs=out_specs, check_vma=False)
```

time: 376 us -> 91.5 us (0.24)
  blocking collectives: 248 us -> 0 us
  Pallas kernels: 0 us -> 87.6 us
  waiting for transfers between devices: 76 us -> 0 us
  matrix products: 33.8 us -> 0 us
  between operations: 14.1 us -> 0.65 us
    psum x2 -> x0, blocking collectives: 151 us -> none  [the longest x1 77 us: shards(): lax.psum(jnp.dot(curvature_product, adapter_second_factor, preferred_elem...]
    pallas_call x0 -> x1, Pallas kernels: none -> 87.6 us  [shards(): pl.pallas_call(kernel, out_shape=(jax.ShapeDtypeStruct((RANK, WIDTH), F32...]
    pmax x1 -> x0, blocking collectives: 77.1 us -> none  [wide_stats(): row_top = lax.pmax(jnp.max(vocab_logits, axis=1), ('dp', 'vocab'))]
    all_gather x1 -> x0, waiting for transfers between devices: 75.3 us -> none  [shards(): lax.all_gather(window_hidden_states, 'dp', axis=0, tiled=True)]
    dot_general x9 -> x0, matrix products: 33.8 us -> none  [the longest x1 12.1 us: output_head_logits(): jnp.dot(states, weights.T, preferred_element_type=jnp.float32)]
    all_gather x2 -> x0, blocking collectives: 19.9 us -> none  [the longest x1 10.6 us: shards(): lax.all_gather(reduced_rank_projection, 'dp', axis=0, tiled=True)]
  transfers between devices with their start and end apart: 1 -> 0, of which waited for: 1 -> 0; matrix products, arithmetic and copies ran while one was open for 1% -> 0% of each run, Pallas kernels for 0% -> 0%
where the time goes in v1:
time: 91.5 us; the launch traced here: 91.4 us
  Pallas kernels  87.6 us (96%)
  local copies, waits for them, and re-layouts  3.09 us (3%)
    pallas_call x1, Pallas kernels, shards(): pl.pallas_call(kernel, out_shape=(jax.ShapeDtypeStruct((RANK, WIDTH), F32...  87.6 us
    unnamed x4, local copies, waits for them, and re-layouts  3.09 us

profile of v1, /device:TPU:1, one launch (start us, length us, event | category | flops | bytes accessed | tf_op | source)
XLA Modules:
  0.0 91.4 jit_solution(17516196481992410515)
XLA Ops:
  0.6 87.6 %shard_map.77 = (f32[64,4608]{1,0:T(8,128)}, f32[64,768]{1,0:T(8,128)}) custom-call(bf16[256,4608]{1,0:T(8,128)(2,1)} %s_ref.1, bf16[768,4608]{1,0:T(8,128)(2,1)} %w_ref.1, bf16[64,4608]{1,0:T(8,128)(2,1)} %a_ref.1, bf16[64,4608]{1,0:T(8,128)(2,1)} %ad_ref.1, bf16[64,768]{1,0:T(8,128)(2,1)} %bitcast.4, bf16[64,768]{1,0:T(8,128)(2,1)} %bitcast.5), custom_call_target="tpu_custom_call" | custom-call | flops 10000000000 | bytes 20000000 | tf_op jit(solution)/shard_map/pallas_call | solution.py:316
  88.3 0.0 copy-start
  88.3 2.4 %copy.10 = f32[64,4608]{1,0:T(8,128)} copy(f32[64,4608]{1,0:T(8,128)} %get-tuple-element.8) | data formatting | bytes 2359296
  90.7 0.0 copy-done
  90.7 0.7 copy.11
Async XLA Ops:
  88.3 2.4 %copy-start = (f32[64,768]{1,0:T(8,128)S(1)}, f32[64,768]{1,0:T(8,128)}, u32[]{:S(2)}) copy-start(f32[64,768]{1,0:T(8,128)} %get-tuple-element.5) | copy-start | bytes 589828

commit v2 on v1

--- a/solution.py
+++ b/solution.py
@@ -16,7 +16,8 @@
 CHUNK = 256
 ROWS = VOCAB + 2 * RANK
 NX, NY, NZ = 4, 4, 8
-DEPTH = 1536
+HALF = 2304
+PART = 64
 BLOCK = 64
 COLS = 512
 
@@ -67,7 +68,7 @@
     s_ref, w_ref, a_ref, ad_ref, bt_ref, dbt_ref, ga_ref, gb_ref,
     wall, sg, acc, e_buf, t_buf, xr, bl, bt2, h1, h2, hs, cfull,
     p0, r1, p1, r2, r3, cg, stg,
-    load_sem, ys, yr, gs, gr, ss1, sr1, xs, xrv, zs, zr, cs, cr, ts, tr, fs, fr,
+    load_sem, ys, yr, ns, nr, gs, gr, ss1, sr1, xs, xrv, zs, zr, cs, cr, ts, tr, fs, fr,
 ):
     y = lax.axis_index("dp")
     v = lax.axis_index("vocab")
@@ -101,48 +102,71 @@
 
     pl.semaphore_wait(barrier, len(everyone))
 
-    half = c * (CHUNK // 2)
-    quarter = CHUNK // 4
+    colour = (x + z) % 2
     before, after, across = (y + 3) % NY, (y + 1) % NY, (y + 2) % NY
-    mine = s_ref.at[pl.ds(pl.multiple_of(half, 16), CHUNK // 2)]
-    sends = [
-        remote(mine, rows_of(y, half, CHUNK // 2), ys.at[0], yr.at[0], y_up),
-        remote(mine, rows_of(y, half, CHUNK // 2), ys.at[1], yr.at[1], y_down),
+    steps = [(before, 0), (after, 1), (before, 1), (after, 0), (across, 0), (across, 1)]
+    around = [
+        place((x + 1) % NX, y, z, c),
+        place((x + 3) % NX, y, z, c),
+        place(x, y, (z + 1) % NZ, c),
+        place(x, y, (z + 7) % NZ, c),
     ]
-    for send in sends:
-        send.start()
+    sends = []
+
+    def send(*args):
+        copy = remote(*args)
+        copy.start()
+        sends.append(copy)
 
     def arrived(ref, send_sem, recv_sem):
         remote(ref, ref, send_sem, recv_sem, sib).wait_recv()
 
-    def pass_on(j, k):
-        held = rows_of(j, half, CHUNK // 2)
-        copy = remote(held, held, gs.at[k], gr.at[k], sib)
-        copy.start()
-        sends.append(copy)
-
-    def whole(j, k):
-        arrived(rows_of(j, CHUNK // 2 - half, CHUNK // 2), gs.at[k], gr.at[k])
-
-    def compute(j):
+    def piece(j, core, shade, h, first=0, size=PART):
+        row = pl.multiple_of(j * CHUNK + (core * 2 + shade) * PART + first, 16)
+        return sg.at[pl.ds(row, size), pl.ds(h * HALF, HALF)]
+
+    def start_y(k, h, device):
+        row = pl.multiple_of((c * 2 + colour) * PART, 16)
+        send(s_ref.at[pl.ds(row, PART), pl.ds(h * HALF, HALF)], piece(y, c, colour, h), ys.at[k], yr.at[k], device)
+
+    def from_y(k):
+        j, h = steps[k]
+        held = piece(j, c, colour, h)
+        arrived(held, ys.at[k], yr.at[k])
+        if k == 0:
+            send(held, held, ys.at[4], yr.at[4], y_up)
+        if k == 1:
+            send(held, held, ys.at[5], yr.at[5], y_down)
+        for i, device in enumerate(around):
+            part = piece(j, c, colour, h, 16 * i, 16)
+            send(part, part, ns.at[k * 4 + i], nr.at[k * 4 + i], device)
+        send(held, held, gs.at[k * 2], gr.at[k * 2], sib)
+
+    def from_around(k):
+        j, h = steps[k]
+        for i in range(4):
+            arrived(piece(j, c, 1 - colour, h, 16 * i, 16), ns.at[k * 4 + i], nr.at[k * 4 + i])
+        held = piece(j, c, 1 - colour, h)
+        send(held, held, gs.at[k * 2 + 1], gr.at[k * 2 + 1], sib)
+
+    def from_sib(k):
+        j, h = steps[k]
+        arrived(piece(j, 1 - c, colour, h), gs.at[k * 2], gr.at[k * 2])
+        arrived(piece(j, 1 - c, 1 - colour, h), gs.at[k * 2 + 1], gr.at[k * 2 + 1])
+
+    start_y(0, 0, y_up)
+    start_y(1, 1, y_down)
+    start_y(2, 1, y_up)
+    start_y(3, 0, y_down)
+
+    def product(j, h):
+        here, at = pl.ds(pl.multiple_of(j * CHUNK, CHUNK), CHUNK), pl.ds(h * HALF, HALF)
+        return lax.dot_general(wall[:, at], sg[here, at], (((1,), (1,)), ((), ())), preferred_element_type=F32)
+
+    def finish(j, acc):
         first = pl.multiple_of(j * CHUNK, CHUNK)
         here = pl.ds(first, CHUNK)
 
-        def deep(k, carry):
-            at = pl.ds(pl.multiple_of(k * DEPTH, 128), DEPTH)
-            part = lax.dot_general(wall[:, at], sg[here, at], (((1,), (1,)), ((), ())), preferred_element_type=F32)
-
-            @pl.when(k == 0)
-            def _():
-                acc[...] = part
-
-            @pl.when(k > 0)
-            def _():
-                acc[...] += part
-
-            return carry
-
-        lax.fori_loop(0, WIDTH // DEPTH, deep, 0)
         xr[:, here] = acc[VOCAB:ROWS, :].astype(BF16)
 
         def logits(i, top):
@@ -186,26 +210,37 @@
 
     for load in loads:
         load.wait()
-    compute(y)
-    arrived(rows_of(before, half, CHUNK // 2), ys.at[0], yr.at[0])
-    held = rows_of(before, half, quarter)
-    sends.append(remote(held, held, ys.at[2], yr.at[2], y_up))
-    sends[-1].start()
-    pass_on(before, 0)
-    arrived(rows_of(after, half, CHUNK // 2), ys.at[1], yr.at[1])
-    held = rows_of(after, half + quarter, quarter)
-    sends.append(remote(held, held, ys.at[3], yr.at[3], y_down))
-    sends[-1].start()
-    pass_on(after, 1)
-    whole(before, 0)
-    compute(before)
-    whole(after, 1)
-    compute(after)
-    arrived(rows_of(across, half, quarter), ys.at[2], yr.at[2])
-    arrived(rows_of(across, half + quarter, quarter), ys.at[3], yr.at[3])
-    pass_on(across, 2)
-    whole(across, 2)
-    compute(across)
+    first_acc, second_acc = acc.at[0], acc.at[1]
+    here = pl.ds(pl.multiple_of(y * CHUNK, CHUNK), CHUNK)
+    first_acc[...] = lax.dot_general(wall[...], sg[here, :], (((1,), (1,)), ((), ())), preferred_element_type=F32)
+    finish(y, first_acc)
+    from_y(0)
+    from_y(1)
+    from_around(0)
+    from_around(1)
+    from_y(2)
+    from_y(3)
+    from_sib(0)
+    first_acc[...] = product(before, 0)
+    from_sib(1)
+    second_acc[...] = product(after, 1)
+    from_around(2)
+    from_around(3)
+    from_y(4)
+    from_y(5)
+    from_sib(2)
+    first_acc[...] += product(before, 1)
+    from_sib(3)
+    second_acc[...] += product(after, 0)
+    finish(before, first_acc)
+    from_around(4)
+    from_around(5)
+    finish(after, second_acc)
+    from_sib(4)
+    first_acc[...] = product(across, 0)
+    from_sib(5)
+    first_acc[...] += product(across, 1)
+    finish(across, first_acc)
 
     copy = remote(p0.at[1 - c], r1, ss1.at[0], sr1.at[0], sib)
     copy.start()
@@ -305,8 +340,8 @@
         return carry
 
     lax.fori_loop(0, WIDTH // COLS, outer, 0)
-    for send in sends:
-        send.wait_send()
+    for copy in sends:
+        copy.wait_send()
 
 
 def shards(states, weight, first, second, first_direction, second_direction):
@@ -321,7 +356,7 @@
         scratch_shapes=[
             pltpu.VMEM((ROWS, WIDTH), BF16),
             pltpu.VMEM((TOKENS, WIDTH), BF16),
-            pltpu.VMEM((ROWS, CHUNK), F32),
+            pltpu.VMEM((2, ROWS, CHUNK), F32),
             pltpu.VMEM((VOCAB, TOKENS), F32),
             pltpu.VMEM((VOCAB, TOKENS), F32),
             pltpu.VMEM((2 * RANK, TOKENS), BF16),
@@ -339,8 +374,9 @@
             pltpu.VMEM((2 * NX, RANK, 128), BF16),
             pltpu.VMEM((2 * NX, 8, 128), F32),
             dma((4,)),
-            dma((4,)), dma((4,)),
-            dma((3,)), dma((3,)),
+            dma((6,)), dma((6,)),
+            dma((24,)), dma((24,)),
+            dma((12,)), dma((12,)),
             dma((1,)), dma((1,)),
             dma((15,)), dma((15,)),
             dma((7,)), dma((7,)),

time: 91.5 us -> 81 us (0.89)
  Pallas kernels: 87.6 us -> 77.1 us
    pallas_call x1, Pallas kernels: 87.6 us -> 77.1 us  [shards(): pl.pallas_call(kernel, out_shape=(jax.ShapeDtypeStruct((RANK, WIDTH), F32...]
where the time goes in v2:
time: 81 us; the launch traced here: 80.8 us
  Pallas kernels  77.1 us (95%)
  local copies, waits for them, and re-layouts  3.09 us (4%)
    pallas_call x1, Pallas kernels, shards(): pl.pallas_call(kernel, out_shape=(jax.ShapeDtypeStruct((RANK, WIDTH), F32...  77.1 us
    unnamed x4, local copies, waits for them, and re-layouts  3.09 us

profile of v2, /device:TPU:1, one launch (start us, length us, event | category | flops | bytes accessed | tf_op | source)
XLA Modules:
  0.0 80.8 jit_solution(5317041126345931638)
XLA Ops:
  0.6 77.1 %shard_map.77 = (f32[64,4608]{1,0:T(8,128)}, f32[64,768]{1,0:T(8,128)}) custom-call(bf16[256,4608]{1,0:T(8,128)(2,1)} %s_ref.1, bf16[768,4608]{1,0:T(8,128)(2,1)} %w_ref.1, bf16[64,4608]{1,0:T(8,128)(2,1)} %a_ref.1, bf16[64,4608]{1,0:T(8,128)(2,1)} %ad_ref.1, bf16[64,768]{1,0:T(8,128)(2,1)} %bitcast.4, bf16[64,768]{1,0:T(8,128)(2,1)} %bitcast.5), custom_call_target="tpu_custom_call" | custom-call | flops 10000000000 | bytes 20000000 | tf_op jit(solution)/shard_map/pallas_call | solution.py:351
  77.7 0.0 copy-start
  77.8 2.4 %copy.10 = f32[64,4608]{1,0:T(8,128)} copy(f32[64,4608]{1,0:T(8,128)} %get-tuple-element.8) | data formatting | bytes 2359296
  80.2 0.0 copy-done
  80.2 0.7 copy.11
Async XLA Ops:
  77.7 2.4 %copy-start = (f32[64,768]{1,0:T(8,128)S(1)}, f32[64,768]{1,0:T(8,128)}, u32[]{:S(2)}) copy-start(f32[64,768]{1,0:T(8,128)} %get-tuple-element.5) | copy-start | bytes 589828

commit v3 on v2

v3 whole, which is shorter than its diff:
```python
import jax
import jax.numpy as jnp
from jax import lax
from jax.experimental import pallas as pl
from jax.experimental.pallas import tpu as pltpu
from jax.sharding import PartitionSpec as P

MESH = pl.DeviceIdType.MESH
F32 = jnp.float32
BF16 = jnp.bfloat16

WIDTH = 4608
RANK = 64
VOCAB = 768
TOKENS = 1024
CHUNK = 256
ROWS = VOCAB + 2 * RANK
NX, NY, NZ = 4, 4, 8
HALF = 2304
PART = 64
BLOCK = 64
COLS = 512


def place(x, y, z, c):
    return (y, x * 16 + z * 2 + c)


def remote(src, dst, send_sem, recv_sem, device):
    return pltpu.make_async_remote_copy(
        src_ref=src,
        dst_ref=dst,
        send_sem=send_sem,
        recv_sem=recv_sem,
        device_id=device,
        device_id_type=MESH,
    )


def merge(parts):
    top = parts[0][0]
    for part in parts[1:]:
        top = jnp.maximum(top, part[0])
    scales = [jnp.exp(part[0] - top) for part in parts]
    total = scales[0] * parts[0][1]
    weighted = total * parts[0][2]
    for scale, part in zip(scales[1:], parts[1:]):
        share = scale * part[1]
        total = total + share
        weighted = weighted + share * part[2]
    mean = weighted / total
    moved = None
    plain = None
    for scale, part in zip(scales, parts):
        shift = scale * (part[2] - mean)
        one = scale * part[3] + shift * part[4]
        two = scale * part[4]
        moved = one if moved is None else moved + one
        plain = two if plain is None else plain + two
    return top, total, mean, moved, plain


def stat_rows(top, total, mean):
    return jnp.concatenate([top, total, mean, jnp.zeros((5, top.shape[1]), F32)], axis=0)


def kernel(
    s_ref, w_ref, a_ref, ad_ref, bt_hbm, dbt_hbm, ga_ref, gb_ref,
    bt_ref, dbt_ref,
    wall, sg, acc, e_buf, t_buf, xr, bl, bt2, h1, h2, hs,
    p0, r1, p1, r2, r3, cg, stg,
    load_sem, ys, yr, ns, nr, gs, gr, ss1, sr1, xs, xrv, zs, zr, cs, cr, ts, tr, fs, fr,
):
    y = lax.axis_index("dp")
    v = lax.axis_index("vocab")
    x, z, c = v // 16, (v // 2) % 8, v % 2
    sib = place(x, y, z, 1 - c)
    y_up, y_down = place(x, (y + 1) % NY, z, c), place(x, (y + 3) % NY, z, c)
    pairs = [(dx, dy) for dx in range(NX) for dy in range(NY) if (dx, dy) != (0, 0)]
    xy = [((x + dx) % NX, (y + dy) % NY) for dx, dy in pairs]

    barrier = pltpu.get_barrier_semaphore()
    everyone = [sib] + [place(px, py, z, c) for px, py in xy] + [place(x, y, (z + d) % NZ, c) for d in range(1, NZ)]
    for peer in everyone:
        pl.semaphore_signal(barrier, 1, device_id=peer, device_id_type=MESH)

    def rows_of(j, start, size):
        return sg.at[pl.ds(pl.multiple_of(j * CHUNK + start, 16), size)]

    loads = [
        pltpu.make_async_copy(s_ref, rows_of(y, 0, CHUNK), load_sem.at[0]),
        pltpu.make_async_copy(w_ref, wall.at[pl.ds(0, VOCAB)], load_sem.at[1]),
        pltpu.make_async_copy(a_ref, wall.at[pl.ds(VOCAB, RANK)], load_sem.at[2]),
        pltpu.make_async_copy(ad_ref, wall.at[pl.ds(VOCAB + RANK, RANK)], load_sem.at[3]),
        pltpu.make_async_copy(bt_hbm, bt_ref, load_sem.at[4]),
        pltpu.make_async_copy(dbt_hbm, dbt_ref, load_sem.at[5]),
    ]
    for load in loads:
        load.start()

    pl.semaphore_wait(barrier, len(everyone))

    colour = (x + z) % 2
    before, after, across = (y + 3) % NY, (y + 1) % NY, (y + 2) % NY
    steps = [(before, 0), (after, 1), (before, 1), (after, 0), (across, 0), (across, 1)]
    around = [
        place((x + 1) % NX, y, z, c),
        place((x + 3) % NX, y, z, c),
        place(x, y, (z + 1) % NZ, c),
        place(x, y, (z + 7) % NZ, c),
    ]
    sends = []

    def send(make):
        make().start()
        sends.append(make)

    def drain():
        for make in sends:
            make().wait_send()
        sends.clear()

    def arrived(ref, send_sem, recv_sem):
        remote(ref, ref, send_sem, recv_sem, sib).wait_recv()

    def piece(j, core, shade, h, first=0, size=PART):
        row = pl.multiple_of(j * CHUNK + (core * 2 + shade) * PART + first, 16)
        return sg.at[pl.ds(row, size), pl.ds(h * HALF, HALF)]

    def start_y(k, h, device):
        def make():
            row = pl.multiple_of((c * 2 + colour) * PART, 16)
            held = s_ref.at[pl.ds(row, PART), pl.ds(h * HALF, HALF)]
            return remote(held, piece(y, c, colour, h), ys.at[k], yr.at[k], device)

        send(make)

    def forward(pick, send_sems, recv_sems, n, device):
        send(lambda: remote(pick(), pick(), send_sems.at[n], recv_sems.at[n], device))

    def from_y(k):
        j, h = steps[k]

        def held():
            return piece(j, c, colour, h)

        arrived(held(), ys.at[k], yr.at[k])
        if k == 0:
            forward(held, ys, yr, 4, y_up)
        if k == 1:
            forward(held, ys, yr, 5, y_down)
        for i, device in enumerate(around):
            n = k * 4 + i
            forward(lambda i=i: piece(j, c, colour, h, 16 * i, 16), ns, nr, n, device)
        forward(held, gs, gr, k * 2, sib)

    def from_around(k):
        j, h = steps[k]
        for i in range(4):
            arrived(piece(j, c, 1 - colour, h, 16 * i, 16), ns.at[k * 4 + i], nr.at[k * 4 + i])
        forward(lambda: piece(j, c, 1 - colour, h), gs, gr, k * 2 + 1, sib)

    def from_sib(k):
        j, h = steps[k]
        arrived(piece(j, 1 - c, colour, h), gs.at[k * 2], gr.at[k * 2])
        arrived(piece(j, 1 - c, 1 - colour, h), gs.at[k * 2 + 1], gr.at[k * 2 + 1])

    start_y(0, 0, y_up)
    start_y(1, 1, y_down)
    start_y(2, 1, y_up)
    start_y(3, 0, y_down)

    def finish(j, acc):
        first = pl.multiple_of(j * CHUNK, CHUNK)
        here = pl.ds(first, CHUNK)

        low = acc[VOCAB:ROWS, :].astype(BF16)
        xr[:, here] = low
        e_buf[:, here] = acc[0:VOCAB, :] + jnp.dot(bl[...], low, preferred_element_type=F32)
        t_buf[:, here] = jnp.dot(bt2[...], low, preferred_element_type=F32)
        blocks = [pl.ds(i, BLOCK) for i in range(0, VOCAB, BLOCK)]

        def fold(values, add):
            return add(values.reshape(BLOCK // 8, 8, CHUNK), axis=0)

        top = fold(e_buf[blocks[0], here], jnp.max)
        for at in blocks[1:]:
            top = jnp.maximum(top, fold(e_buf[at, here], jnp.max))
        top = jnp.max(top, axis=0, keepdims=True)
        total = jnp.zeros((8, CHUNK), F32)
        weighted = jnp.zeros((8, CHUNK), F32)
        for at in blocks:
            e = jnp.exp(e_buf[at, here] - top)
            e_buf[at, here] = e
            h2[at, :] = e.astype(BF16)
            total = total + fold(e, jnp.sum)
            weighted = weighted + fold(e * t_buf[at, here], jnp.sum)
        total = jnp.sum(total, axis=0, keepdims=True)
        mean = jnp.sum(weighted, axis=0, keepdims=True) / total
        for at in blocks:
            h1[at, :] = (e_buf[at, here] * (t_buf[at, here] - mean)).astype(BF16)
        side, there = j // 2, pl.ds(pl.multiple_of((j % 2) * CHUNK, CHUNK), CHUNK)
        p0[side, 0:RANK, there] = jnp.dot(bt_ref[...], h1[...], preferred_element_type=F32)
        p0[side, RANK : 2 * RANK, there] = jnp.dot(bt_ref[...], h2[...], preferred_element_type=F32)
        p0[side, 2 * RANK : 2 * RANK + 8, there] = stat_rows(top, total, mean)

    for load in loads:
        load.wait()
    bt = bt_ref[...].astype(F32)
    dbt = dbt_ref[...].astype(F32)
    bl[...] = jnp.concatenate([bt, jnp.zeros_like(bt)], axis=0).T.astype(BF16)
    bt2[...] = jnp.concatenate([dbt, bt], axis=0).T.astype(BF16)

    def any_of(i, *values):
        hit = i == values[0]
        for value in values[1:]:
            hit = hit | (i == value)
        return hit

    def work(i, carry):
        @pl.when(i == 2)
        def _():
            from_y(0)
            from_y(1)
            from_around(0)
            from_around(1)
            from_y(2)
            from_y(3)
            from_sib(0)

        @pl.when(i == 3)
        def _():
            from_sib(1)

        @pl.when(i == 4)
        def _():
            from_around(2)
            from_around(3)
            from_y(4)
            from_y(5)
            from_sib(2)

        @pl.when(i == 5)
        def _():
            from_sib(3)

        @pl.when(i == 6)
        def _():
            from_sib(4)

        @pl.when(i == 7)
        def _():
            from_sib(5)

        step = jnp.where(i < 2, 0, jnp.where(any_of(i, 2, 4), 3, jnp.where(i < 6, 1, 2)))
        j = (y + step) % NY
        h = jnp.where(any_of(i, 1, 3, 4, 7), 1, 0)
        total = acc.at[jnp.where(step == 1, 1, 0)]
        here = pl.ds(pl.multiple_of(j * CHUNK, CHUNK), CHUNK)
        at = pl.ds(pl.multiple_of(h * HALF, 128), HALF)
        part = lax.dot_general(wall[:, at], sg[here, at], (((1,), (1,)), ((), ())), preferred_element_type=F32)
        fresh = any_of(i, 0, 2, 3, 6)

        @pl.when(fresh)
        def _():
            total[...] = part

        @pl.when(jnp.logical_not(fresh))
        def _():
            total[...] += part

        @pl.when(i == 5)
        def _():
            from_around(4)
            from_around(5)

        @pl.when(any_of(i, 1, 4, 5, 7))
        def _():
            finish(j, total)

        return carry

    lax.fori_loop(0, 8, work, 0)

    send(lambda: remote(p0.at[1 - c], r1, ss1.at[0], sr1.at[0], sib))
    arrived(r1, ss1.at[0], sr1.at[0])
    for tx in range(NX):
        lanes = pl.ds(tx * 128, 128)

        def stats(ref, row):
            return ref[pl.ds(row, 1), lanes]

        own, other = p0.at[c], r1
        for ty in range(NY):
            g1, g2 = pl.ds(ty * 16, 16), pl.ds(RANK + ty * 16, 16)
            out = merge(
                [
                    (stats(ref, 128), stats(ref, 129), stats(ref, 130), ref[g1, lanes], ref[g2, lanes])
                    for ref in (own, other)
                ]
            )
            p1[tx * NY + ty] = jnp.concatenate([out[3], out[4], stat_rows(*out[:3])], axis=0)

    def unpack(ref, k):
        return (ref[k, 32:33], ref[k, 33:34], ref[k, 34:35], ref[k, 0:16], ref[k, 16:32])

    me = x * NY + y
    early = list(sends)
    sends.clear()
    for k, (px, py) in enumerate(xy):
        send(
            lambda k=k, px=px, py=py: remote(
                p1.at[px * NY + py], r2.at[me], xs.at[k], xrv.at[k], place(px, py, z, c)
            )
        )
    for make in early:
        make().wait_send()
    r2[me] = p1[me]
    for k, (dx, dy) in enumerate(pairs):
        origin = ((x - dx + NX) % NX) * NY + (y - dy + NY) % NY
        arrived(r2.at[origin], xs.at[k], xrv.at[k])
    out = merge([unpack(r2, k) for k in range(NX * NY)])
    r3[z] = jnp.concatenate([out[3], out[4], stat_rows(*out[:3])], axis=0)
    for d in range(1, NZ):
        forward(lambda: r3.at[z], zs, zr, d - 1, place(x, y, (z + d) % NZ, c))
    for d in range(1, NZ):
        arrived(r3.at[(z - d + NZ) % NZ], zs.at[d - 1], zr.at[d - 1])
    top, total, mean, moved, plain = merge([unpack(r3, k) for k in range(NZ)])

    slot = c * NX + x
    strip = cg.at[slot, pl.ds(pl.multiple_of(y * 16, 16), 16)]
    strip[...] = (moved / total).astype(BF16)
    stg[slot] = stat_rows(top, total, mean)
    for d in range(1, NX):
        forward(lambda: stg.at[slot], ts, tr, d - 1, place((x + d) % NX, y, z, c))
    for k, (px, py) in enumerate(xy):
        forward(lambda: strip, cs, cr, k, place(px, py, z, c))
    for d in range(1, NX):
        arrived(stg.at[c * NX + (x - d + NX) % NX], ts.at[d - 1], tr.at[d - 1])
    forward(lambda: stg.at[pl.ds(c * NX, NX)], fs, fr, 0, sib)
    for k, (dx, dy) in enumerate(pairs):
        from_x, from_y = (x - dx + NX) % NX, (y - dy + NY) % NY
        arrived(cg.at[c * NX + from_x, pl.ds(pl.multiple_of(from_y * 16, 16), 16)], cs.at[k], cr.at[k])
    forward(lambda: cg.at[pl.ds(c * NX, NX)], fs, fr, 1, sib)
    arrived(stg.at[pl.ds((1 - c) * NX, NX)], fs.at[0], fr.at[0])

    factors, means = [], []
    for t in range(8):
        local_top = p0[t // 4, 128:129, (t % 4) * 128 : (t % 4 + 1) * 128]
        factors.append(jnp.exp(local_top - stg[t, 0:1]) / stg[t, 1:2])
        means.append(stg[t, 2:3])

    def hessian(i, carry):
        at = pl.ds(pl.multiple_of(i * BLOCK, BLOCK), BLOCK)
        for t in range(8):
            lanes = pl.ds(t * 128, 128)
            probs = e_buf[at, lanes] * factors[t]
            hs[at, lanes] = (probs * (t_buf[at, lanes] - means[t])).astype(BF16)
        return carry

    lax.fori_loop(0, VOCAB // BLOCK, hessian, 0)
    gb_ref[...] = lax.dot_general(xr[0:RANK, :], hs[...], (((1,), (1,)), ((), ())), preferred_element_type=F32)

    def outer(core, first):
        rows = pl.ds(pl.multiple_of(core * (TOKENS // 2), TOKENS // 2), TOKENS // 2)
        lows = jnp.concatenate([cg[core * NX + t] for t in range(NX)], axis=1)

        def columns(n, carry):
            at = pl.ds(pl.multiple_of(n * COLS, 128), COLS)
            part = jnp.dot(lows, sg[rows, at], preferred_element_type=F32)
            ga_ref[:, at] = part if first else ga_ref[:, at] + part
            return carry

        lax.fori_loop(0, WIDTH // COLS, columns, 0)

    outer(c, True)
    arrived(cg.at[pl.ds((1 - c) * NX, NX)], fs.at[1], fr.at[1])
    outer(1 - c, False)
    drain()


def shards(states, weight, first, second, first_direction, second_direction):
    vmem = pl.BlockSpec(memory_space=pltpu.VMEM)
    hbm = pl.BlockSpec(memory_space=pl.ANY)
    dma = pltpu.SemaphoreType.DMA
    grad_a, grad_b = pl.pallas_call(
        kernel,
        out_shape=(pltpu.VMEM((RANK, WIDTH), F32), pltpu.VMEM((RANK, VOCAB), F32)),
        in_specs=[hbm] * 6,
        out_specs=(vmem, vmem),
        scratch_shapes=[
            pltpu.VMEM((RANK, VOCAB), BF16),
            pltpu.VMEM((RANK, VOCAB), BF16),
            pltpu.VMEM((ROWS, WIDTH), BF16),
            pltpu.VMEM((TOKENS, WIDTH), BF16),
            pltpu.VMEM((2, ROWS, CHUNK), F32),
            pltpu.VMEM((VOCAB, TOKENS), F32),
            pltpu.VMEM((VOCAB, TOKENS), F32),
            pltpu.VMEM((2 * RANK, TOKENS), BF16),
            pltpu.VMEM((VOCAB, 2 * RANK), BF16),
            pltpu.VMEM((VOCAB, 2 * RANK), BF16),
            pltpu.VMEM((VOCAB, CHUNK), BF16),
            pltpu.VMEM((VOCAB, CHUNK), BF16),
            pltpu.VMEM((VOCAB, TOKENS), BF16),
            pltpu.VMEM((2, 2 * RANK + 8, TOKENS // 2), F32),
            pltpu.VMEM((2 * RANK + 8, TOKENS // 2), F32),
            pltpu.VMEM((NX * NY, 40, 128), F32),
            pltpu.VMEM((NX * NY, 40, 128), F32),
            pltpu.VMEM((NZ, 40, 128), F32),
            pltpu.VMEM((2 * NX, RANK, 128), BF16),
            pltpu.VMEM((2 * NX, 8, 128), F32),
            dma((6,)),
            dma((6,)), dma((6,)),
            dma((24,)), dma((24,)),
            dma((12,)), dma((12,)),
            dma((1,)), dma((1,)),
            dma((15,)), dma((15,)),
            dma((7,)), dma((7,)),
            dma((15,)), dma((15,)),
            dma((3,)), dma((3,)),
            dma((2,)), dma((2,)),
        ],
        compiler_params=pltpu.CompilerParams(
            collective_id=0, has_side_effects=True, vmem_limit_bytes=56 * 1024 * 1024
        ),
        cost_estimate=pl.CostEstimate(flops=10_000_000_000, bytes_accessed=20_000_000, transcendentals=800_000),
    )(states, weight, first, first_direction, second.T, second_direction.T)
    return grad_a, grad_b.T


def solution(mesh):
    in_specs = (
        P("dp", None),
        P(("dp", "vocab"), None),
        P(),
        P(("dp", "vocab"), None),
        P(),
        P(("dp", "vocab"), None),
    )
    out_specs = (P(), P(("dp", "vocab"), None))
    return jax.shard_map(shards, mesh=mesh, in_specs=in_specs, out_specs=out_specs, check_vma=False)
```

time: 81 us -> 69.8 us (0.86)
  Pallas kernels: 77.1 us -> 67.4 us
  local copies, waits for them, and re-layouts: 3.09 us -> 1.69 us
    pallas_call x1, Pallas kernels: 77.1 us -> 67.4 us  [shards(): pl.pallas_call(kernel, out_shape=(pltpu.VMEM((RANK, WIDTH), F32), pltpu.V...]
    unnamed x4 -> x2, local copies, waits for them, and re-layouts: 3.09 us -> 1.69 us
where the time goes in v3:
time: 69.8 us; the launch traced here: 69.7 us
  Pallas kernels  67.4 us (97%)
  local copies, waits for them, and re-layouts  1.69 us (2%)
    pallas_call x1, Pallas kernels, shards(): pl.pallas_call(kernel, out_shape=(pltpu.VMEM((RANK, WIDTH), F32), pltpu.V...  67.4 us
    unnamed x2, local copies, waits for them, and re-layouts  1.69 us

profile of v3, /device:TPU:1, one launch (start us, length us, event | category | flops | bytes accessed | tf_op | source)
XLA Modules:
  0.0 69.7 jit_solution(11951719487792541999)
XLA Ops:
  0.6 67.4 %shard_map.77 = (f32[64,4608]{1,0:T(8,128)S(1)}, f32[64,768]{1,0:T(8,128)S(1)}) custom-call(bf16[256,4608]{1,0:T(8,128)(2,1)} %s_ref.1, bf16[768,4608]{1,0:T(8,128)(2,1)} %w_ref.1, bf16[64,4608]{1,0:T(8,128)(2,1)} %a_ref.1, bf16[64,4608]{1,0:T(8,128)(2,1)} %ad_ref.1, bf16[64,768]{1,0:T(8,128)(2,1)} %bitcast.4, bf16[64,768]{1,0:T(8,128)(2,1)} %bitcast.5), custom_call_target="tpu_custom_call" | custom-call | flops 10000000000 | bytes 20000000 | tf_op jit(solution)/shard_map/pallas_call | solution.py:386
  68.0 1.0 %copy.10 = f32[64,4608]{1,0:T(8,128)} copy(f32[64,4608]{1,0:T(8,128)S(1)} %get-tuple-element.6) | data formatting | bytes 2359296
  69.0 0.7 copy.11

commit v4 on v3

--- a/solution.py
+++ b/solution.py
@@ -17,7 +17,7 @@
 ROWS = VOCAB + 2 * RANK
 NX, NY, NZ = 4, 4, 8
 HALF = 2304
-PART = 64
+QUARTER = 1152
 BLOCK = 64
 COLS = 512
 
@@ -81,6 +81,7 @@
 
     barrier = pltpu.get_barrier_semaphore()
     everyone = [sib] + [place(px, py, z, c) for px, py in xy] + [place(x, y, (z + d) % NZ, c) for d in range(1, NZ)]
+    everyone += [place((x + dx) % NX, y, (z + dz) % NZ, c) for dx in (1, 3) for dz in (1, 7)]
     for peer in everyone:
         pl.semaphore_signal(barrier, 1, device_id=peer, device_id_type=MESH)
 
@@ -100,8 +101,14 @@
 
     pl.semaphore_wait(barrier, len(everyone))
 
+    odd = x % 2
     colour = (x + z) % 2
+    lead, rest, wide = colour * 64 + odd * 32, colour * 64 + 32 - odd * 16, colour * 64 + 32 - odd * 32
+    corner, missing = colour * 64 + odd * 48, colour * 64 + (1 - odd) * 48
+    other = (1 - colour) * 64
+    other_x, other_z = other + (1 - odd) * 32, other + odd * 32
     before, after, across = (y + 3) % NY, (y + 1) % NY, (y + 2) % NY
+    whole = (2, 3)
     steps = [(before, 0), (after, 1), (before, 1), (after, 0), (across, 0), (across, 1)]
     around = [
         place((x + 1) % NX, y, z, c),
@@ -109,6 +116,10 @@
         place(x, y, (z + 1) % NZ, c),
         place(x, y, (z + 7) % NZ, c),
     ]
+    corners = [
+        [place((x + 1) % NX, y, (z + 1) % NZ, c), place((x + 3) % NX, y, (z + 7) % NZ, c)],
+        [place((x + 1) % NX, y, (z + 7) % NZ, c), place((x + 3) % NX, y, (z + 1) % NZ, c)],
+    ]
     sends = []
 
     def send(make):
@@ -123,15 +134,15 @@
     def arrived(ref, send_sem, recv_sem):
         remote(ref, ref, send_sem, recv_sem, sib).wait_recv()
 
-    def piece(j, core, shade, h, first=0, size=PART):
-        row = pl.multiple_of(j * CHUNK + (core * 2 + shade) * PART + first, 16)
-        return sg.at[pl.ds(row, size), pl.ds(h * HALF, HALF)]
-
-    def start_y(k, h, device):
+    def piece(j, core, first, size, column, width=HALF):
+        row = pl.multiple_of(j * CHUNK + core * (CHUNK // 2) + first, 16)
+        return sg.at[pl.ds(row, size), pl.ds(column, width)]
+
+    def start_y(k, h, first, size, device):
         def make():
-            row = pl.multiple_of((c * 2 + colour) * PART, 16)
-            held = s_ref.at[pl.ds(row, PART), pl.ds(h * HALF, HALF)]
-            return remote(held, piece(y, c, colour, h), ys.at[k], yr.at[k], device)
+            row = pl.multiple_of(c * (CHUNK // 2) + first, 16)
+            held = s_ref.at[pl.ds(row, size), pl.ds(h * HALF, HALF)]
+            return remote(held, piece(y, c, first, size, h * HALF), ys.at[k], yr.at[k], device)
 
         send(make)
 
@@ -140,35 +151,59 @@
 
     def from_y(k):
         j, h = steps[k]
+        left = h * HALF
 
         def held():
-            return piece(j, c, colour, h)
+            return piece(j, c, lead, 32, left)
 
         arrived(held(), ys.at[k], yr.at[k])
-        if k == 0:
-            forward(held, ys, yr, 4, y_up)
-        if k == 1:
-            forward(held, ys, yr, 5, y_down)
         for i, device in enumerate(around):
-            n = k * 4 + i
-            forward(lambda i=i: piece(j, c, colour, h, 16 * i, 16), ns, nr, n, device)
-        forward(held, gs, gr, k * 2, sib)
+            column = left + (i % 2) * QUARTER
+            forward(lambda column=column: piece(j, c, lead, 32, column, QUARTER), ns, nr, k * 6 + i, device)
+        for i, device in enumerate([] if k in whole else corners[h]):
+            column = left + i * QUARTER
+            forward(lambda column=column: piece(j, c, corner, 16, column, QUARTER), ns, nr, k * 6 + 4 + i, device)
+        if k < 2:
+            forward(held, ys, yr, k + 4, (y_up, y_down)[k])
+        forward(held, gs, gr, k * 4, sib)
+
+    def rest_y(k):
+        j, h = steps[k]
+
+        def held():
+            return piece(j, c, wide, 32, h * HALF) if k in whole else piece(j, c, rest, 16, h * HALF)
+
+        arrived(held(), ys.at[k + 6], yr.at[k + 6])
+        if k < 2:
+            forward(held, ys, yr, k + 10, (y_up, y_down)[k])
+        forward(held, gs, gr, k * 4 + 3, sib)
 
     def from_around(k):
         j, h = steps[k]
+        left = h * HALF
         for i in range(4):
-            arrived(piece(j, c, 1 - colour, h, 16 * i, 16), ns.at[k * 4 + i], nr.at[k * 4 + i])
-        forward(lambda: piece(j, c, 1 - colour, h), gs, gr, k * 2 + 1, sib)
+            first = other_x if i < 2 else other_z
+            n = k * 6 + i
+            arrived(piece(j, c, first, 32, left + (i % 2) * QUARTER, QUARTER), ns.at[n], nr.at[n])
+        forward(lambda: piece(j, c, other, 64, left), gs, gr, k * 4 + 1, sib)
+        if k in whole:
+            return
+        for i in range(2):
+            n = k * 6 + 4 + i
+            arrived(piece(j, c, missing, 16, left + i * QUARTER, QUARTER), ns.at[n], nr.at[n])
+        forward(lambda: piece(j, c, missing, 16, left), gs, gr, k * 4 + 2, sib)
 
     def from_sib(k):
         j, h = steps[k]
-        arrived(piece(j, 1 - c, colour, h), gs.at[k * 2], gr.at[k * 2])
-        arrived(piece(j, 1 - c, 1 - colour, h), gs.at[k * 2 + 1], gr.at[k * 2 + 1])
-
-    start_y(0, 0, y_up)
-    start_y(1, 1, y_down)
-    start_y(2, 1, y_up)
-    start_y(3, 0, y_down)
+        parts = [(0, lead, 32), (1, other, 64)]
+        parts += [(3, wide, 32)] if k in whole else [(2, missing, 16), (3, rest, 16)]
+        for i, first, size in parts:
+            arrived(piece(j, 1 - c, first, size, h * HALF), gs.at[k * 4 + i], gr.at[k * 4 + i])
+
+    for k, (h, device) in enumerate([(0, y_up), (1, y_down), (1, y_up), (0, y_down)]):
+        start_y(k, h, lead, 32, device)
+    for k, (h, device) in enumerate([(0, y_up), (1, y_down)]):
+        start_y(6 + k, h, rest, 16, device)
 
     def finish(j, acc):
         first = pl.multiple_of(j * CHUNK, CHUNK)
@@ -218,14 +253,23 @@
         return hit
 
     def work(i, carry):
-        @pl.when(i == 2)
+        @pl.when(i == 1)
         def _():
             from_y(0)
             from_y(1)
+            start_y(8, 1, wide, 32, y_up)
+            start_y(9, 0, wide, 32, y_down)
+
+        @pl.when(i == 2)
+        def _():
+            from_y(2)
+            from_y(3)
+            rest_y(0)
+            rest_y(1)
             from_around(0)
             from_around(1)
-            from_y(2)
-            from_y(3)
+            from_y(4)
+            from_y(5)
             from_sib(0)
 
         @pl.when(i == 3)
@@ -234,10 +278,10 @@
 
         @pl.when(i == 4)
         def _():
+            rest_y(2)
+            rest_y(3)
             from_around(2)
             from_around(3)
-            from_y(4)
-            from_y(5)
             from_sib(2)
 
         @pl.when(i == 5)
@@ -269,9 +313,14 @@
         def _():
             total[...] += part
 
+        @pl.when(i == 4)
+        def _():
+            rest_y(4)
+            rest_y(5)
+            from_around(4)
+
         @pl.when(i == 5)
         def _():
-            from_around(4)
             from_around(5)
 
         @pl.when(any_of(i, 1, 4, 5, 7))
@@ -290,13 +339,13 @@
         def stats(ref, row):
             return ref[pl.ds(row, 1), lanes]
 
-        own, other = p0.at[c], r1
+        ours, theirs = p0.at[c], r1
         for ty in range(NY):
             g1, g2 = pl.ds(ty * 16, 16), pl.ds(RANK + ty * 16, 16)
             out = merge(
                 [
                     (stats(ref, 128), stats(ref, 129), stats(ref, 130), ref[g1, lanes], ref[g2, lanes])
-                    for ref in (own, other)
+                    for ref in (ours, theirs)
                 ]
             )
             p1[tx * NY + ty] = jnp.concatenate([out[3], out[4], stat_rows(*out[:3])], axis=0)
@@ -338,28 +387,34 @@
     for d in range(1, NX):
         arrived(stg.at[c * NX + (x - d + NX) % NX], ts.at[d - 1], tr.at[d - 1])
     forward(lambda: stg.at[pl.ds(c * NX, NX)], fs, fr, 0, sib)
+
+    def curve(core, first):
+        tiles = [(pl.ds(pl.multiple_of(core * 512 + t * 128, 128), 128), core * NX + t) for t in range(NX)]
+        factors, means = [], []
+        for t, (lanes, k) in enumerate(tiles):
+            local_top = p0[core, 2 * RANK : 2 * RANK + 1, t * 128 : (t + 1) * 128]
+            factors.append(jnp.exp(local_top - stg[k, 0:1]) / stg[k, 1:2])
+            means.append(stg[k, 2:3])
+
+        def hessian(i, carry):
+            at = pl.ds(pl.multiple_of(i * BLOCK, BLOCK), BLOCK)
+            for t, (lanes, k) in enumerate(tiles):
+                probs = e_buf[at, lanes] * factors[t]
+                hs[at, lanes] = (probs * (t_buf[at, lanes] - means[t])).astype(BF16)
+            return carry
+
+        lax.fori_loop(0, VOCAB // BLOCK, hessian, 0)
+        at = pl.ds(pl.multiple_of(core * 512, 512), 512)
+        part = lax.dot_general(xr[0:RANK, at], hs[:, at], (((1,), (1,)), ((), ())), preferred_element_type=F32)
+        gb_ref[...] = part if first else gb_ref[...] + part
+
+    curve(c, True)
     for k, (dx, dy) in enumerate(pairs):
-        from_x, from_y = (x - dx + NX) % NX, (y - dy + NY) % NY
-        arrived(cg.at[c * NX + from_x, pl.ds(pl.multiple_of(from_y * 16, 16), 16)], cs.at[k], cr.at[k])
+        at_x, at_y = (x - dx + NX) % NX, (y - dy + NY) % NY
+        arrived(cg.at[c * NX + at_x, pl.ds(pl.multiple_of(at_y * 16, 16), 16)], cs.at[k], cr.at[k])
     forward(lambda: cg.at[pl.ds(c * NX, NX)], fs, fr, 1, sib)
     arrived(stg.at[pl.ds((1 - c) * NX, NX)], fs.at[0], fr.at[0])
-
-    factors, means = [], []
-    for t in range(8):
-        local_top = p0[t // 4, 128:129, (t % 4) * 128 : (t % 4 + 1) * 128]
-        factors.append(jnp.exp(local_top - stg[t, 0:1]) / stg[t, 1:2])
-        means.append(stg[t, 2:3])
-
-    def hessian(i, carry):
-        at = pl.ds(pl.multiple_of(i * BLOCK, BLOCK), BLOCK)
-        for t in range(8):
-            lanes = pl.ds(t * 128, 128)
-            probs = e_buf[at, lanes] * factors[t]
-            hs[at, lanes] = (probs * (t_buf[at, lanes] - means[t])).astype(BF16)
-        return carry
-
-    lax.fori_loop(0, VOCAB // BLOCK, hessian, 0)
-    gb_ref[...] = lax.dot_general(xr[0:RANK, :], hs[...], (((1,), (1,)), ((), ())), preferred_element_type=F32)
+    curve(1 - c, False)
 
     def outer(core, first):
         rows = pl.ds(pl.multiple_of(core * (TOKENS // 2), TOKENS // 2), TOKENS // 2)
@@ -410,9 +465,9 @@
             pltpu.VMEM((2 * NX, RANK, 128), BF16),
             pltpu.VMEM((2 * NX, 8, 128), F32),
             dma((6,)),
-            dma((6,)), dma((6,)),
+            dma((12,)), dma((12,)),
+            dma((36,)), dma((36,)),
             dma((24,)), dma((24,)),
-            dma((12,)), dma((12,)),
             dma((1,)), dma((1,)),
             dma((15,)), dma((15,)),
             dma((7,)), dma((7,)),

time: 69.8 us -> 67.5 us (0.967)
  Pallas kernels: 67.4 us -> 65 us
    pallas_call x1, Pallas kernels: 67.4 us -> 65 us  [shards(): pl.pallas_call(kernel, out_shape=(pltpu.VMEM((RANK, WIDTH), F32), pltpu.V...]
where the time goes in v4:
time: 67.5 us; the launch traced here: 67.4 us
  Pallas kernels  65 us (96%)
  local copies, waits for them, and re-layouts  1.69 us (3%)
    pallas_call x1, Pallas kernels, shards(): pl.pallas_call(kernel, out_shape=(pltpu.VMEM((RANK, WIDTH), F32), pltpu.V...  65 us
    unnamed x2, local copies, waits for them, and re-layouts  1.69 us

profile of v4, /device:TPU:1, one launch (start us, length us, event | category | flops | bytes accessed | tf_op | source)
XLA Modules:
  0.0 67.4 jit_solution(10209377579990104982)
XLA Ops:
  0.6 65.0 %shard_map.77 = (f32[64,4608]{1,0:T(8,128)S(1)}, f32[64,768]{1,0:T(8,128)S(1)}) custom-call(bf16[256,4608]{1,0:T(8,128)(2,1)} %s_ref.1, bf16[768,4608]{1,0:T(8,128)(2,1)} %w_ref.1, bf16[64,4608]{1,0:T(8,128)(2,1)} %a_ref.1, bf16[64,4608]{1,0:T(8,128)(2,1)} %ad_ref.1, bf16[64,768]{1,0:T(8,128)(2,1)} %bitcast.4, bf16[64,768]{1,0:T(8,128)(2,1)} %bitcast.5), custom_call_target="tpu_custom_call" | custom-call | flops 10000000000 | bytes 20000000 | tf_op jit(solution)/shard_map/pallas_call | solution.py:441
  65.7 1.0 %copy.10 = f32[64,4608]{1,0:T(8,128)} copy(f32[64,4608]{1,0:T(8,128)S(1)} %get-tuple-element.6) | data formatting | bytes 2359296
  66.7 0.7 %copy.11 = f32[768,64]{0,1:T(8,128)} copy(f32[768,64]{0,1:T(8,128)S(1)} %bitcast.3) | data formatting | bytes 393216

commit v5 on v4

--- a/solution.py
+++ b/solution.py
@@ -64,6 +64,32 @@
     return jnp.concatenate([top, total, mean, jnp.zeros((5, top.shape[1]), F32)], axis=0)
 
 
+def pack(top, total, mean, moved, plain):
+    stats = jnp.concatenate([top, total, mean], axis=0)
+    high = stats.astype(BF16).astype(F32)
+    middle = (stats - high).astype(BF16).astype(F32)
+    low = stats - high - middle
+    blank = jnp.zeros((7, top.shape[1]), F32)
+    return jnp.concatenate([moved, plain, high, middle, low, blank], axis=0).astype(BF16)
+
+
+def unpack(ref, k):
+    block = ref[k].astype(F32)
+    stats = block[32:35] + block[35:38] + block[38:41]
+    return stats[0:1], stats[1:2], stats[2:3], block[0:16], block[16:32]
+
+
+def store(a_ref, b_ref, a_out, b_out, sems):
+    copies = [
+        pltpu.make_async_copy(a_ref, a_out, sems.at[0]),
+        pltpu.make_async_copy(b_ref, b_out, sems.at[1]),
+    ]
+    for copy in copies:
+        copy.start()
+    for copy in copies:
+        copy.wait()
+
+
 def kernel(
     s_ref, w_ref, a_ref, ad_ref, bt_hbm, dbt_hbm, ga_ref, gb_ref,
     bt_ref, dbt_ref,
@@ -80,8 +106,11 @@
     xy = [((x + dx) % NX, (y + dy) % NY) for dx, dy in pairs]
 
     barrier = pltpu.get_barrier_semaphore()
-    everyone = [sib] + [place(px, py, z, c) for px, py in xy] + [place(x, y, (z + d) % NZ, c) for d in range(1, NZ)]
+    everyone = [y_up, y_down, sib]
+    everyone += [place((x + dx) % NX, y, z, c) for dx in (1, 3)]
+    everyone += [place(x, y, (z + d) % NZ, c) for d in range(1, NZ)]
     everyone += [place((x + dx) % NX, y, (z + dz) % NZ, c) for dx in (1, 3) for dz in (1, 7)]
+    everyone += [place(px, py, z, c) for (dx, dy), (px, py) in zip(pairs, xy) if (dx, dy) not in ((0, 1), (0, 3), (1, 0), (3, 0))]
     for peer in everyone:
         pl.semaphore_signal(barrier, 1, device_id=peer, device_id_type=MESH)
 
@@ -348,10 +377,7 @@
                     for ref in (ours, theirs)
                 ]
             )
-            p1[tx * NY + ty] = jnp.concatenate([out[3], out[4], stat_rows(*out[:3])], axis=0)
-
-    def unpack(ref, k):
-        return (ref[k, 32:33], ref[k, 33:34], ref[k, 34:35], ref[k, 0:16], ref[k, 16:32])
+            p1[tx * NY + ty] = pack(*out)
 
     me = x * NY + y
     early = list(sends)
@@ -369,7 +395,7 @@
         origin = ((x - dx + NX) % NX) * NY + (y - dy + NY) % NY
         arrived(r2.at[origin], xs.at[k], xrv.at[k])
     out = merge([unpack(r2, k) for k in range(NX * NY)])
-    r3[z] = jnp.concatenate([out[3], out[4], stat_rows(*out[:3])], axis=0)
+    r3[z] = pack(*out)
     for d in range(1, NZ):
         forward(lambda: r3.at[z], zs, zr, d - 1, place(x, y, (z + d) % NZ, c))
     for d in range(1, NZ):
@@ -380,10 +406,14 @@
     strip = cg.at[slot, pl.ds(pl.multiple_of(y * 16, 16), 16)]
     strip[...] = (moved / total).astype(BF16)
     stg[slot] = stat_rows(top, total, mean)
+    early = list(sends)
+    sends.clear()
     for d in range(1, NX):
         forward(lambda: stg.at[slot], ts, tr, d - 1, place((x + d) % NX, y, z, c))
     for k, (px, py) in enumerate(xy):
         forward(lambda: strip, cs, cr, k, place(px, py, z, c))
+    for make in early:
+        make().wait_send()
     for d in range(1, NX):
         arrived(stg.at[c * NX + (x - d + NX) % NX], ts.at[d - 1], tr.at[d - 1])
     forward(lambda: stg.at[pl.ds(c * NX, NX)], fs, fr, 0, sib)
@@ -459,9 +489,9 @@
             pltpu.VMEM((VOCAB, TOKENS), BF16),
             pltpu.VMEM((2, 2 * RANK + 8, TOKENS // 2), F32),
             pltpu.VMEM((2 * RANK + 8, TOKENS // 2), F32),
-            pltpu.VMEM((NX * NY, 40, 128), F32),
-            pltpu.VMEM((NX * NY, 40, 128), F32),
-            pltpu.VMEM((NZ, 40, 128), F32),
+            pltpu.VMEM((NX * NY, 48, 128), BF16),
+            pltpu.VMEM((NX * NY, 48, 128), BF16),
+            pltpu.VMEM((NZ, 48, 128), BF16),
             pltpu.VMEM((2 * NX, RANK, 128), BF16),
             pltpu.VMEM((2 * NX, 8, 128), F32),
             dma((6,)),

time: 67.5 us -> 64.8 us (0.960)
  Pallas kernels: 65 us -> 62.4 us
    pallas_call x1, Pallas kernels: 65 us -> 62.4 us  [shards(): pl.pallas_call(kernel, out_shape=(pltpu.VMEM((RANK, WIDTH), F32), pltpu.V...]
where the time goes in v5:
time: 64.8 us
  Pallas kernels  62.4 us (96%)
  local copies, waits for them, and re-layouts  1.69 us (3%)
    pallas_call x1, Pallas kernels, shards(): pl.pallas_call(kernel, out_shape=(pltpu.VMEM((RANK, WIDTH), F32), pltpu.V...  62.4 us
    unnamed x2, local copies, waits for them, and re-layouts  1.69 us

profile of v5, /device:TPU:1, one launch (start us, length us, event | category | flops | bytes accessed | tf_op | source)
XLA Modules:
  0.0 64.8 jit_solution(14225006445934911582)
XLA Ops:
  0.6 62.4 %shard_map.77 = (f32[64,4608]{1,0:T(8,128)S(1)}, f32[64,768]{1,0:T(8,128)S(1)}) custom-call(bf16[256,4608]{1,0:T(8,128)(2,1)} %s_ref.1, bf16[768,4608]{1,0:T(8,128)(2,1)} %w_ref.1, bf16[64,4608]{1,0:T(8,128)(2,1)} %a_ref.1, bf16[64,4608]{1,0:T(8,128)(2,1)} %ad_ref.1, bf16[64,768]{1,0:T(8,128)(2,1)} %bitcast.4, bf16[64,768]{1,0:T(8,128)(2,1)} %bitcast.5), custom_call_target="tpu_custom_call" | custom-call | flops 10000000000 | bytes 20000000 | tf_op jit(solution)/shard_map/pallas_call | solution.py:471
  63.1 1.0 %copy.10 = f32[64,4608]{1,0:T(8,128)} copy(f32[64,4608]{1,0:T(8,128)S(1)} %get-tuple-element.6) | data formatting | bytes 2359296
  64.1 0.7 %copy.11 = f32[768,64]{0,1:T(8,128)} copy(f32[768,64]{0,1:T(8,128)S(1)} %bitcast.3) | data formatting | bytes 393216

commit v6 on v5

--- a/solution.py
+++ b/solution.py
@@ -19,7 +19,7 @@
 HALF = 2304
 QUARTER = 1152
 BLOCK = 64
-COLS = 512
+COLS = 2304
 
 
 def place(x, y, z, c):

time: 64.8 us -> 63.3 us (0.977)
  Pallas kernels: 62.4 us -> 60.8 us
    pallas_call x1, Pallas kernels: 62.4 us -> 60.8 us  [shards(): pl.pallas_call(kernel, out_shape=(pltpu.VMEM((RANK, WIDTH), F32), pltpu.V...]
where the time goes in v6:
time: 63.3 us; the launch traced here: 63.2 us
  Pallas kernels  60.8 us (96%)
  local copies, waits for them, and re-layouts  1.69 us (3%)
  between operations  0.64 us (1%)
    pallas_call x1, Pallas kernels, shards(): pl.pallas_call(kernel, out_shape=(pltpu.VMEM((RANK, WIDTH), F32), pltpu.V...  60.8 us
    unnamed x2, local copies, waits for them, and re-layouts  1.69 us

profile of v6, /device:TPU:1, one launch (start us, length us, event | category | flops | bytes accessed | tf_op | source)
XLA Modules:
  0.0 63.2 jit_solution(4901386959410657328)
XLA Ops:
  0.6 60.8 %shard_map.77 = (f32[64,4608]{1,0:T(8,128)S(1)}, f32[64,768]{1,0:T(8,128)S(1)}) custom-call(bf16[256,4608]{1,0:T(8,128)(2,1)} %s_ref.1, bf16[768,4608]{1,0:T(8,128)(2,1)} %w_ref.1, bf16[64,4608]{1,0:T(8,128)(2,1)} %a_ref.1, bf16[64,4608]{1,0:T(8,128)(2,1)} %ad_ref.1, bf16[64,768]{1,0:T(8,128)(2,1)} %bitcast.4, bf16[64,768]{1,0:T(8,128)(2,1)} %bitcast.5), custom_call_target="tpu_custom_call" | custom-call | flops 10000000000 | bytes 20000000 | tf_op jit(solution)/shard_map/pallas_call | solution.py:471
  61.5 1.0 %copy.10 = f32[64,4608]{1,0:T(8,128)} copy(f32[64,4608]{1,0:T(8,128)S(1)} %get-tuple-element.6) | data formatting | bytes 2359296
  62.5 0.7 %copy.11 = f32[768,64]{0,1:T(8,128)} copy(f32[768,64]{0,1:T(8,128)S(1)} %bitcast.3) | data formatting | bytes 393216

commit v7 on v6

--- a/solution.py
+++ b/solution.py
@@ -103,6 +103,7 @@
     sib = place(x, y, z, 1 - c)
     y_up, y_down = place(x, (y + 1) % NY, z, c), place(x, (y + 3) % NY, z, c)
     pairs = [(dx, dy) for dx in range(NX) for dy in range(NY) if (dx, dy) != (0, 0)]
+    pairs.sort(key=lambda pair: -min(pair[0], NX - pair[0]) - min(pair[1], NY - pair[1]))
     xy = [((x + dx) % NX, (y + dy) % NY) for dx, dy in pairs]
 
     barrier = pltpu.get_barrier_semaphore()
@@ -396,7 +397,7 @@
         arrived(r2.at[origin], xs.at[k], xrv.at[k])
     out = merge([unpack(r2, k) for k in range(NX * NY)])
     r3[z] = pack(*out)
-    for d in range(1, NZ):
+    for d in (4, 3, 5, 2, 6, 1, 7):
         forward(lambda: r3.at[z], zs, zr, d - 1, place(x, y, (z + d) % NZ, c))
     for d in range(1, NZ):
         arrived(r3.at[(z - d + NZ) % NZ], zs.at[d - 1], zr.at[d - 1])

time: 63.3 us -> 62.5 us (0.987)
  Pallas kernels: 60.8 us -> 60.1 us
    pallas_call x1, Pallas kernels: 60.8 us -> 60.1 us  [shards(): pl.pallas_call(kernel, out_shape=(pltpu.VMEM((RANK, WIDTH), F32), pltpu.V...]
where the time goes in v7:
time: 62.5 us; the launch traced here: 62.4 us
  Pallas kernels  60.1 us (96%)
  local copies, waits for them, and re-layouts  1.69 us (3%)
  between operations  0.64 us (1%)
    pallas_call x1, Pallas kernels, shards(): pl.pallas_call(kernel, out_shape=(pltpu.VMEM((RANK, WIDTH), F32), pltpu.V...  60.1 us
    unnamed x2, local copies, waits for them, and re-layouts  1.69 us

profile of v7, /device:TPU:1, one launch (start us, length us, event | category | flops | bytes accessed | tf_op | source)
XLA Modules:
  0.0 62.4 jit_solution(18306013502434057505)
XLA Ops:
  0.6 60.1 %shard_map.77 = (f32[64,4608]{1,0:T(8,128)S(1)}, f32[64,768]{1,0:T(8,128)S(1)}) custom-call(bf16[256,4608]{1,0:T(8,128)(2,1)} %s_ref.1, bf16[768,4608]{1,0:T(8,128)(2,1)} %w_ref.1, bf16[64,4608]{1,0:T(8,128)(2,1)} %a_ref.1, bf16[64,4608]{1,0:T(8,128)(2,1)} %ad_ref.1, bf16[64,768]{1,0:T(8,128)(2,1)} %bitcast.4, bf16[64,768]{1,0:T(8,128)(2,1)} %bitcast.5), custom_call_target="tpu_custom_call" | custom-call | flops 10000000000 | bytes 20000000 | tf_op jit(solution)/shard_map/pallas_call | solution.py:472
  60.7 1.0 %copy.10 = f32[64,4608]{1,0:T(8,128)} copy(f32[64,4608]{1,0:T(8,128)S(1)} %get-tuple-element.6) | data formatting | bytes 2359296
  61.7 0.7 %copy.11 = f32[768,64]{0,1:T(8,128)} copy(f32[768,64]{0,1:T(8,128)S(1)} %bitcast.3) | data formatting | bytes 393216
